TPU v7x, 512 devices: a whole 4x8x8 slice. The times are simulated.
512 devices in a mesh: rng: 64 (over y_lo, x, z), chan: 8 (over y_hi, core).
Axes of the slice: x: 4, y: 8 (y_hi: 4, y_lo: 2; y = y_hi * 2 + y_lo), z: 8, core: 2. Of those that a mesh axis runs over, the one named last changes fastest.
Arguments:
- samples: bfloat16 [2, 4, 512, 32768], P(None, None, 'chan', 'rng'), may hold values from -6 to 6
- phase_codes: int32 [16, 128], replicated, may hold values from 0 to 15
- block_pattern: int32 [16, 8], replicated, may hold values 0 or 1
- steering: bfloat16 [2, 8, 64], replicated, may hold values from -0.75 to 0.75
Outputs:
- normalized: float32 [8, 512, 32768], P('chan', 'rng')
All inputs are finite; a program needn't handle non-finite values.
Results may differ from a plain program's by a relative error of at most 0.015.
Values may be sent and summed in bfloat16 or wider, within the bound.
A program may use at most 64 MiB of HBM per device.

v0:
```python
import math

import jax
import jax.numpy as jnp
from jax import lax
from jax.sharding import PartitionSpec as P

PHASES = 16


def passed_along(block, axis, distance):
    devices = range(lax.axis_size(axis))
    route = [(i - distance, i) for i in devices if i - distance in devices]
    return lax.ppermute(block, axis, route)


def banded(code_rows, chip_count):
    tx_count = code_rows.shape[0]
    padding = jnp.zeros((tx_count, chip_count + 1), code_rows.dtype)
    period = jnp.concatenate([code_rows, padding], axis=1)
    tiled = jnp.tile(period, (1, chip_count))[:, : 2 * chip_count * chip_count]
    shifted = tiled.reshape(tx_count, chip_count, 2 * chip_count)
    return jnp.swapaxes(shifted, 1, 2)


def code_filter(phase_codes, block_pattern, chip_count):
    tx_count, block_count = block_pattern.shape
    per_block = chip_count // block_count
    pattern = block_pattern.astype(jnp.float32)[:, :, None]
    active = jnp.broadcast_to(pattern, (tx_count, block_count, per_block)).reshape(
        tx_count, chip_count
    )
    code_phase = phase_codes.astype(jnp.float32) * (2.0 * math.pi / PHASES)
    code_re = (jnp.cos(code_phase) * active).astype(jnp.bfloat16)
    code_im = (jnp.sin(code_phase) * active).astype(jnp.bfloat16)
    real_part = banded(code_re, chip_count)
    imag_part = banded(code_im, chip_count)
    upper_rows = jnp.concatenate([real_part, imag_part], axis=1)
    lower_rows = jnp.concatenate([-imag_part, real_part], axis=1)
    return jnp.stack([upper_rows, lower_rows])


def doppler(series):
    pulse_count = series.shape[2]
    bin_iota = lax.broadcasted_iota(jnp.int32, (pulse_count, pulse_count), 0)
    time_iota = lax.broadcasted_iota(jnp.int32, (pulse_count, pulse_count), 1)
    angles = (bin_iota * time_iota % pulse_count).astype(jnp.float32) * (
        2.0 * math.pi / pulse_count
    )
    cosine = jnp.cos(angles)
    sine = jnp.sin(angles)
    dft_table = jnp.stack([jnp.stack([cosine, sine]), jnp.stack([-sine, cosine])])
    table_high = dft_table.astype(jnp.bfloat16)
    table_low = (dft_table - table_high.astype(jnp.float32)).astype(jnp.bfloat16)
    result = jnp.einsum("cdkp,dbpg->cbkg", table_high, series, preferred_element_type=jnp.float32)
    result = result + jnp.einsum(
        "cdkp,dbpg->cbkg", table_low, series, preferred_element_type=jnp.float32
    )
    return result.astype(jnp.bfloat16)


def local(samples, phase_codes, block_pattern, steering):
    tx_count, chip_count = phase_codes.shape
    rx_count = samples.shape[1]
    pulse_count = samples.shape[2]
    gate_count = samples.shape[3]
    block_count = gate_count // chip_count
    edge_cells = passed_along(samples[:, :, :, :chip_count], "rng", -1)
    extended = jnp.concatenate([samples, edge_cells], axis=3)
    leading = extended[:, :, :, :gate_count].reshape(
        2, rx_count, pulse_count, block_count, chip_count
    )
    trailing = extended[:, :, :, chip_count:].reshape(
        2, rx_count, pulse_count, block_count, chip_count
    )
    windows = jnp.concatenate([leading, trailing], axis=4)
    stacked = jnp.concatenate([windows[0], windows[1]], axis=3)
    filters = code_filter(phase_codes, block_pattern, chip_count)
    matched = jnp.einsum(
        "rpms,ctsg->crtpmg", stacked, filters, preferred_element_type=jnp.float32
    ).astype(jnp.bfloat16)
    matched = matched.reshape(2, rx_count * tx_count, pulse_count, gate_count)
    weight_re = steering[0]
    weight_im = steering[1]
    mixer = jnp.stack([jnp.stack([weight_re, -weight_im]), jnp.stack([weight_im, weight_re])])
    beams = jnp.einsum(
        "cdbq,dqpg->cbpg", mixer, matched, preferred_element_type=jnp.float32
    ).astype(jnp.bfloat16)
    spectrum = doppler(lax.all_to_all(beams, "chan", split_axis=1, concat_axis=2, tiled=True))
    turned = lax.all_to_all(spectrum, "rng", split_axis=2, concat_axis=3, tiled=True)
    components = turned.astype(jnp.float32)
    power = (components[0] * components[0] + components[1] * components[1]).astype(jnp.bfloat16)
    levels = power.astype(jnp.float32)
    average = jnp.mean(levels, axis=2, keepdims=True)
    return levels / (average + 1e-06)


def solution(mesh):
    return jax.shard_map(
        local,
        mesh=mesh,
        in_specs=(P(None, None, "chan", "rng"), P(), P(), P()),
        out_specs=P("chan", "rng", None),
        check_vma=False,
    )
```

profile of v0, /device:TPU:1, one launch (start us, length us, event | category | flops | bytes accessed | tf_op | source)
XLA Modules:
  0.0 145.7 jit_solution(8989520573185677179)
XLA Ops:
  0.0 0.9 slice.38
  0.9 1.3 collective-permute-start
  2.2 2.0 %bitcast_dynamic-update-slice_fusion.1 = bf16[2,4,64,4,256]{4,2,3,1,0:T(8,128)(2,1)} fusion(bf16[2,4,64,512]{3,2,1,0:T(8,128)(2,1)} %param.4), kind=kLoop, calls=%fused_computation.36 | loop fusion | bytes 1048576
  4.2 0.7 convert_element_type.119
  4.9 0.1 copy.18
  5.0 0.1 broadcast_in_dim.2
  5.1 0.1 reshape.207
  5.1 0.8 multiply_convert_fusion
  5.9 0.1 tile.20
  6.1 1.8 %tile.21 = bf16[16,32896]{1,0:T(8,128)(2,1)S(1)} reshape(bf16[16,128,257]{2,1,0:T(8,128)(2,1)S(1)} %tile.20) | data formatting | bytes 2105344 | tf_op jit(solution)/shard_map/tile | solution.py:21
  7.9 0.1 slice.45
  8.0 0.2 copy.46
  8.2 0.7 copy.20
  8.9 1.1 bitcast_negate_fusion
  10.0 0.1 tile.8
  10.2 2.6 %tile.9 = bf16[16,32896]{1,0:T(8,128)(2,1)} reshape(bf16[16,128,257]{2,1,0:T(8,128)(2,1)S(1)} %tile.8) | data formatting | bytes 2105344 | tf_op jit(solution)/shard_map/tile | solution.py:21
  12.8 1.2 slice-done
  14.0 1.2 copy.45
  15.2 1.6 %copy.19 = bf16[16,128,256]{1,2,0:T(8,128)(2,1)S(1)} copy(bf16[16,128,256]{2,1,0:T(8,128)(2,1)} %bitcast.90) | data formatting | bytes 2097152 | tf_op jit(solution)/shard_map/reshape | solution.py:22
  16.8 0.0 copy-done.4
  16.9 0.0 copy-done.1
  16.9 0.0 copy-start.2
  16.9 0.0 copy-start.3
  16.9 0.3 maximum_bitcast_fusion.2
  17.2 0.0 collective-permute-done
  17.2 0.7 copy-done.2
  17.9 0.3 copy-done.3
  18.3 0.2 bitcast_dynamic-update-slice_fusion
  18.5 0.1 slice_bitcast_fusion.1
  18.5 5.0 %convert_bitcast_fusion = bf16[2,4,16,64,4,128]{5,3,4,1,2,0:T(8,128)(2,1)S(1)} fusion(bf16[1,16,512,128]{3,2,1,0:T(8,128)(2,1)S(1)} %get-tuple-element.12, bf16[1,16,512,128]{3,2,1,0:T(8,128)(2,1)S(1)} %get-tuple-element.11, bf16[4,64,4,256]{3,1,2,0:T(8,128)(2,1)S(1)} %get-tuple-element.10, bf16[4,64,4,256]{3,1,2,0:T(8,128)(2,1)S(1)} %get-tuple-element.9), kind=kOutput, calls=%fused_computation | convolution fusion | flops 4309647360 | bytes 13631488 | tf_op jit(solution)/shard_map/rpms,ctsg->crtpmg/dot_general | solution.py:79
  23.6 18.5 %copy.39 = bf16[2,4,16,64,4,128]{5,4,2,1,0,3:T(4,128)(2,1)} copy(bf16[2,4,16,64,4,128]{5,3,4,1,2,0:T(8,128)(2,1)S(1)} %convert_bitcast_fusion) | data formatting | bytes 16777216 | tf_op jit(solution)/shard_map/reshape | solution.py:82
  42.0 13.1 %reshape.220 = bf16[2,64,64,512,1]{3,1,0,2,4:T(8,128)(2,1)} reshape(bf16[2,4,16,64,4,128]{5,4,2,1,0,3:T(4,128)(2,1)} %copy.39) | data formatting | bytes 16777216 | tf_op jit(solution)/shard_map/reshape | solution.py:82
  55.2 4.6 %bitcast_convert_fusion = bf16[2,8,64,512]{3,1,2,0:T(8,128)(2,1)S(1)} fusion(bf16[2,64,64,512,1]{3,1,0,2,4:T(8,128)(2,1)} %reshape.220, bf16[1,2,8,64]{3,2,1,0:T(8,128)(2,1)S(1)} %get-tuple-element.19, bf16[1,2,8,64]{3,2,1,0:T(8,128)(2,1)S(1)} %get-tuple-element.18), kind=kOutput, calls=%fused_computation.15 | convolution fusion | flops 134750208 | bytes 9441280 | tf_op jit(solution)/shard_map/cdbq,dqpg->cbpg/dot_general | solution.py:86
  59.8 1.3 copy.25
  61.1 10.3 %all-to-all-start = ((bf16[2,8,64,512]{3,2,0,1:T(8,128)(2,1)}), bf16[2,8,64,512]{3,2,0,1:T(8,128)(2,1)S(1)}, u32[]{:S(2)}, u32[]{:S(2)}) async-start(bf16[2,8,64,512]{3,2,0,1:T(8,128)(2,1)} %copy.25), calls=%async_computation | async-start | bytes 2097152 | tf_op jit(solution)/shard_map/all_to_all | solution.py:89
  71.4 3.9 %fusion.26 = f32[1,512,512]{2,1,0:T(8,128)S(1)} fusion(), kind=kLoop, calls=%fused_computation.44 | loop fusion | flops 3932160 | bytes 1048576 | tf_op jit(solution)/shard_map/neg | solution.py:52
  75.3 4.1 %fusion.24 = (f32[1,512,512]{2,1,0:T(8,128)S(1)}, f32[1,512,512]{2,1,0:T(8,128)S(1)}) fusion(), kind=kLoop, calls=%fused_computation.42 | loop fusion | flops 3670016 | bytes 2097152 | tf_op jit(solution)/shard_map/sin | solution.py:51
  79.4 1.9 %maximum_bitcast_fusion.4 = (f32[1,2,512,512]{3,2,1,0:T(8,128)S(1)}, f32[1,2,512,512]{3,2,1,0:T(8,128)}) fusion(f32[1,512,512]{2,1,0:T(8,128)S(1)} %get-tuple-element.20, f32[1,512,512]{2,1,0:T(8,128)S(1)} %get-tuple-element.21, f32[1,512,512]{2,1,0:T(8,128)S(1)} %fusion.26), kind=kLoop, calls=%fused_computation.10 | loop fusion | flops 1048576 | bytes 7340032 | tf_op jit(solution)/shard_map/stack | solution.py:52
  81.3 11.7 %all-to-all-done = bf16[2,8,64,512]{3,2,0,1:T(8,128)(2,1)S(1)} async-done(((bf16[2,8,64,512]{3,2,0,1:T(8,128)(2,1)}), bf16[2,8,64,512]{3,2,0,1:T(8,128)(2,1)S(1)}, u32[]{:S(2)}, u32[]{:S(2)}) %all-to-all-start) | async-done | bytes 1048608 | tf_op jit(solution)/shard_map/all_to_all | solution.py:89
  93.0 0.1 copy.26
  93.1 1.5 %copy-done = f32[1,2,512,512]{3,2,1,0:T(8,128)S(1)} copy-done((f32[1,2,512,512]{3,2,1,0:T(8,128)S(1)}, f32[1,2,512,512]{3,2,1,0:T(8,128)}, u32[]{:S(2)}) %copy-start) | copy-done | bytes 2097176
  94.6 1.3 fusion.6
  96.0 1.3 fusion.9
  97.3 1.0 copy.29
  98.3 45.5 %all_to_all.8 = bf16[2,1,512,512]{3,0,1,2:T(2,128)(2,1)S(1)} all-to-all(bf16[2,1,512,512]{3,0,1,2:T(2,128)(2,1)S(1)} %copy.29), channel_id=1, replica_groups=mesh['rng'=64,'chan'=8] {'rng'}, dimensions={2} | all-to-all | bytes 2097152 | tf_op jit(solution)/shard_map/all_to_all | solution.py:90
  143.8 0.3 convert_bitcast_fusion.1
  144.1 0.4 fusion.33
  144.6 1.1 broadcast_divide_fusion
  (9 shorter events, 0.0 us)
Async XLA Ops:
  0.9 16.3 %collective-permute-start = (bf16[2,4,64,128]{3,2,1,0:T(8,128)(2,1)S(1)}, bf16[2,4,64,128]{3,2,1,0:T(8,128)(2,1)S(1)}, u32[]{:S(2)}, u32[]{:S(2)}) collective-permute-start(bf16[2,4,64,128]{3,2,1,0:T(8,128)(2,1)S(1)} %slice.38), channel_id=1, source_target_pairs={{8,0},{16,8},{24,16},{32,24},{40,32},{48,40},{56,48},{64,56},{72,6... | collective-permute-start | bytes 393224 | tf_op jit(solution)/shard_map/ppermute | solution.py:14
  12.8 1.2 slice-start
  14.0 2.8 %copy-start.4 = (bf16[2,8,64]{2,1,0:T(8,128)(2,1)S(1)}, bf16[2,8,64]{2,1,0:T(8,128)(2,1)}, u32[]{:S(2)}) copy-start(bf16[2,8,64]{2,1,0:T(8,128)(2,1)} %param.7) | copy-start | bytes 6148
  14.0 2.8 %copy-start.1 = (bf16[16,256,128]{2,1,0:T(8,128)(2,1)S(1)}, bf16[16,256,128]{2,1,0:T(8,128)(2,1)}, u32[]{:S(2)}) copy-start(bf16[16,256,128]{2,1,0:T(8,128)(2,1)} %bitcast_negate_fusion) | copy-start | bytes 3145732
  16.9 1.0 copy-start.2
  16.9 1.4 copy-start.3
  61.1 31.9 %all-to-all-start = ((bf16[2,8,64,512]{3,2,0,1:T(8,128)(2,1)}), bf16[2,8,64,512]{3,2,0,1:T(8,128)(2,1)S(1)}, u32[]{:S(2)}, u32[]{:S(2)}) async-start(bf16[2,8,64,512]{3,2,0,1:T(8,128)(2,1)} %copy.25), calls=%async_computation | async-start | bytes 2097152 | tf_op jit(solution)/shard_map/all_to_all | solution.py:89
  93.0 1.6 %copy-start = (f32[1,2,512,512]{3,2,1,0:T(8,128)S(1)}, f32[1,2,512,512]{3,2,1,0:T(8,128)}, u32[]{:S(2)}) copy-start(f32[1,2,512,512]{3,2,1,0:T(8,128)} %get-tuple-element.8) | copy-start | bytes 6291460
where the time goes:
time: 148 us; the launch traced here: 146 us
  local copies, waits for them, and re-layouts  49.5 us (33%)
  blocking collectives  45.5 us (31%)
  other arithmetic  14.8 us (10%)
  matrix products  12.3 us (8%)
  waiting for transfers between devices  11.7 us (8%)
  starting transfers between devices  11.6 us (8%)
    all_to_all x1, blocking collectives, local(): lax.all_to_all(spectrum, 'rng', split_axis=2, concat_axis=3, tiled=True)  45.5 us
    reshape x2, local copies, waits for them, and re-layouts, local(): matched = matched.reshape(2, rx_count * tx_count, pulse_count, gate_count)  31.6 us
    all_to_all x1, waiting for transfers between devices, local(): lax.all_to_all(beams, 'chan', split_axis=1, concat_axis=2, tiled=True)  11.7 us
    all_to_all x1, starting transfers between devices, local(): lax.all_to_all(beams, 'chan', split_axis=1, concat_axis=2, tiled=True)  10.3 us
    unnamed x13, local copies, waits for them, and re-layouts  6.01 us
    dot_general x1, matrix products, local(): jnp.einsum('rpms,ctsg->crtpmg', stacked, filters, preferred_element_type=...  5.02 us
    another operation x4, local copies, waits for them, and re-layouts, banded(): tiled = jnp.tile(period, (1, chip_count))[:, :2 * chip_count * chip_count]  4.76 us
    dot_general x1, matrix products, local(): jnp.einsum('cdbq,dqpg->cbpg', mixer, matched, preferred_element_type=jnp....  4.62 us
  transfers between devices with their start and end apart: 2, of which 1 were waited for; matrix products, arithmetic and copies ran while one was open for 16% of the time, Pallas kernels for 0%

commit v1 on v0

v1 whole, which is shorter than its diff:
```python
import functools
import math

import jax
import jax.numpy as jnp
import numpy as np
from jax import lax
from jax.experimental import pallas as pl
from jax.experimental.pallas import tpu as pltpu
from jax.sharding import PartitionSpec as P

PHASES = 16
LANES = 128
MESH = pl.DeviceIdType.MESH


def dft_table(pulse_count):
    index = np.arange(pulse_count)
    angles = (np.outer(index, index) % pulse_count) * (2.0 * math.pi / pulse_count)
    cosine, sine = np.cos(angles), np.sin(angles)
    table = np.concatenate(
        [np.concatenate([cosine, sine], axis=1), np.concatenate([-sine, cosine], axis=1)]
    )
    return jnp.asarray(table, jnp.bfloat16)


def dot(left, right):
    return jnp.dot(left, right, preferred_element_type=jnp.float32)


def kernel(
    rng_count,
    chan_count,
    samples_ref,
    codes_ref,
    pattern_ref,
    steering_ref,
    table_hbm,
    out_ref,
    extended,
    table,
    taps,
    filters,
    lines,
    outgoing,
    gathered,
    power_out,
    power_in,
    load_sem,
    table_sem,
    edge_sem,
    beam_send,
    beam_recv,
    power_send,
    power_recv,
):
    rng = lax.axis_index("rng")
    chan = lax.axis_index("chan")
    rx_count, pulses, gates = samples_ref.shape[1:]
    chips = codes_ref.shape[1]
    chunks = outgoing.shape[0]
    width = outgoing.shape[4]
    per_chunk = width // LANES
    bins = table.shape[0] // 2
    own_bins = bins // rng_count

    load = pltpu.make_async_copy(samples_ref, extended.at[:, :, :, pl.ds(0, gates)], load_sem)
    load.start()
    table_load = pltpu.make_async_copy(table_hbm, table, table_sem)
    table_load.start()

    barrier = pltpu.get_barrier_semaphore()

    @pl.loop(1, chan_count)
    def _(step):
        peer = lax.rem(chan + step, chan_count)
        pl.semaphore_signal(barrier, inc=1, device_id={"chan": peer}, device_id_type=MESH)

    @pl.loop(1, rng_count)
    def _(step):
        peer = lax.rem(rng + step, rng_count)
        pl.semaphore_signal(barrier, inc=1, device_id={"rng": peer}, device_id_type=MESH)

    tx_count, block_count = pattern_ref.shape
    spread = (
        lax.broadcasted_iota(jnp.int32, (block_count, chips), 1) // (chips // block_count)
        == lax.broadcasted_iota(jnp.int32, (block_count, chips), 0)
    ).astype(jnp.float32)
    active = dot(pattern_ref[...].astype(jnp.float32), spread)
    phase = codes_ref[...].astype(jnp.float32) * (2.0 * math.pi / PHASES)
    code_re = (jnp.cos(phase) * active).astype(jnp.bfloat16)
    code_im = (jnp.sin(phase) * active).astype(jnp.bfloat16)
    reverse = (
        lax.rem(
            lax.broadcasted_iota(jnp.int32, (chips, 2 * chips), 0)
            + lax.broadcasted_iota(jnp.int32, (chips, 2 * chips), 1),
            2 * chips,
        )
        == 0
    ).astype(jnp.bfloat16)
    back_re = dot(code_re, reverse)
    back_im = dot(code_im, reverse)
    weights = steering_ref[...]
    beam_count = weights.shape[0] // 2
    row = lax.broadcasted_iota(jnp.int32, (rx_count * tx_count, 2 * chips), 0) // tx_count
    for rx in range(rx_count):
        wide_re = jnp.where(row == rx, jnp.concatenate([back_re] * rx_count, 0), 0.0)
        wide_im = jnp.where(row == rx, jnp.concatenate([back_im] * rx_count, 0), 0.0)
        by_re = dot(weights, wide_re.astype(jnp.bfloat16))
        by_im = dot(weights, wide_im.astype(jnp.bfloat16))
        taps[2 * rx] = by_re[:beam_count] + by_im[beam_count:]
        taps[2 * rx + 1] = by_re[beam_count:] - by_im[:beam_count]

    load.wait()

    def fill_lines(chunk):
        for part in range(2):
            for block in range(per_chunk):
                at = (chunk * per_chunk + block) * LANES
                top = (part * per_chunk + block) * pulses
                for rx in range(rx_count):
                    lines[pl.ds(top, pulses), pl.ds(rx * 2 * LANES, 2 * LANES)] = extended[
                        part, rx, :, pl.ds(at, 2 * LANES)
                    ]

    def fill_filter(beam):
        rows = taps[:, pl.ds(beam, 1), :]
        slanted = pltpu.roll(
            jnp.broadcast_to(rows, (2 * rx_count, 8, 2 * chips)), 0, 2, stride=1, stride_axis=1
        )
        for pair in range(chips // 16):
            first = pltpu.roll(slanted, 16 * pair, 2) if pair else slanted
            second = pltpu.roll(slanted, 16 * pair + 8, 2)
            both = jnp.concatenate([first, second], axis=1).astype(jnp.bfloat16)
            for rx in range(rx_count):
                for part in range(2):
                    for half in range(2):
                        filters[
                            beam,
                            pl.ds(rx * 2 * chips + half * chips + 16 * pair, 16),
                            pl.ds(part * LANES, LANES),
                        ] = both[2 * rx + part, :, half * LANES : (half + 1) * LANES]

    def form_beam(beam):
        mixed = dot(lines[...], filters[beam])
        rows = per_chunk * pulses
        real = mixed[:rows, :LANES] - mixed[rows:, LANES:]
        imag = mixed[rows:, :LANES] + mixed[:rows, LANES:]
        return real.astype(jnp.bfloat16), imag.astype(jnp.bfloat16)

    def put(target, values, top):
        for part in range(2):
            for block in range(per_chunk):
                target[part, pl.ds(top, pulses), pl.ds(block * LANES, LANES)] = values[part][
                    block * pulses : (block + 1) * pulses
                ]

    mine = pl.ds(pl.multiple_of(chan * pulses, pulses), pulses)

    def beam_copy(chunk, beam):
        return pltpu.make_async_remote_copy(
            src_ref=outgoing.at[chunk, beam],
            dst_ref=gathered.at[chunk, :, mine, :],
            send_sem=beam_send.at[chunk],
            recv_sem=beam_recv.at[chunk],
            device_id={"chan": beam},
            device_id_type=MESH,
        )

    def partner(step):
        return lax.rem(chan // 2 + step % 4, chan_count // 2) * 2 + (chan + step // 4) % 2

    fill_lines(0)
    pl.semaphore_wait(barrier, rng_count + chan_count - 2)

    edge = pltpu.make_async_remote_copy(
        src_ref=extended.at[:, :, :, pl.ds(0, LANES)],
        dst_ref=extended.at[:, :, :, pl.ds(gates, LANES)],
        send_sem=edge_sem.at[0],
        recv_sem=edge_sem.at[1],
        device_id={"rng": lax.rem(rng + rng_count - 1, rng_count)},
        device_id_type=MESH,
    )
    edge.start()

    for chunk in range(chunks):
        if chunk:
            if chunk == chunks - 1:
                edge.wait()
                tail = extended[:, :, :, pl.ds(gates, LANES)]
                extended[:, :, :, pl.ds(gates, LANES)] = jnp.where(
                    rng == rng_count - 1, jnp.zeros_like(tail), tail
                )
            fill_lines(chunk)

        @pl.loop(1, chan_count)
        def _(step):
            beam = partner(step)
            if chunk == 0:
                fill_filter(beam)
            put(outgoing.at[chunk, beam], form_beam(beam), 0)
            beam_copy(chunk, beam).start()

        if chunk == 0:
            fill_filter(chan)
        put(gathered.at[chunk], form_beam(chan), pl.multiple_of(chan * pulses, pulses))

    def power_copy(chunk, peer):
        return pltpu.make_async_remote_copy(
            src_ref=power_out.at[chunk, peer],
            dst_ref=power_in.at[chunk, rng],
            send_sem=power_send.at[chunk],
            recv_sem=power_recv.at[chunk],
            device_id={"rng": peer},
            device_id_type=MESH,
        )

    table_load.wait()
    step_bins = 128
    for chunk in range(chunks):
        arrived = outgoing.at[chunk, pl.ds(0, chan_count - 1)]
        pltpu.make_async_copy(arrived, arrived, beam_recv.at[chunk]).wait()
        series = jnp.concatenate([gathered[chunk, 0], gathered[chunk, 1]], axis=0)
        for at in range(0, bins, step_bins):
            real = dot(table[pl.ds(at, step_bins), :], series)
            imag = dot(table[pl.ds(bins + at, step_bins), :], series)
            real = real.astype(jnp.bfloat16).astype(jnp.float32)
            imag = imag.astype(jnp.bfloat16).astype(jnp.float32)
            power = (real * real + imag * imag).reshape(step_bins // own_bins, own_bins, width)
            power = jnp.concatenate(
                [power[:, :, i * LANES : (i + 1) * LANES] for i in range(per_chunk)], axis=1
            )
            power_out[chunk, pl.ds(at // own_bins, step_bins // own_bins)] = power.astype(
                jnp.bfloat16
            )

        @pl.loop(1, rng_count)
        def _(step):
            power_copy(chunk, lax.rem(rng + step, rng_count)).start()

        power_in[chunk, rng] = power_out[chunk, rng]

    total = jnp.zeros((own_bins, LANES), jnp.float32)
    for chunk in range(chunks):
        arrived = power_in.at[chunk, pl.ds(0, rng_count - 1)]
        pltpu.make_async_copy(arrived, arrived, power_recv.at[chunk]).wait()
        level = power_in[chunk].astype(jnp.float32)
        level = jnp.sum(level, axis=0)
        for i in range(per_chunk):
            total = total + level[i * own_bins : (i + 1) * own_bins]
    average = jnp.sum(total, axis=1, keepdims=True) / float(rng_count * gates)
    scale = 1.0 / (average + 1e-06)
    for source in range(rng_count):
        for chunk in range(chunks):
            level = power_in[chunk, source].astype(jnp.float32)
            for i in range(per_chunk):
                out_ref[
                    0, :, pl.ds(source * gates + chunk * width + i * LANES, LANES)
                ] = level[i * own_bins : (i + 1) * own_bins] * scale

    for chunk in range(chunks):
        sent = outgoing.at[chunk, pl.ds(0, chan_count - 1)]
        pltpu.make_async_copy(sent, sent, beam_send.at[chunk]).wait()
        sent = power_out.at[chunk, pl.ds(0, rng_count - 1)]
        pltpu.make_async_copy(sent, sent, power_send.at[chunk]).wait()


def local(rng_count, chan_count, samples, phase_codes, block_pattern, steering):
    _, rx_count, pulses, gates = samples.shape
    chips = phase_codes.shape[1]
    _, beam_count, pair_count = steering.shape
    bins = pulses * chan_count
    own_bins = bins // rng_count
    chunks = 2
    width = gates // chunks
    per_chunk = width // LANES
    vmem = pl.BlockSpec(memory_space=pltpu.VMEM)
    hbm = pl.BlockSpec(memory_space=pl.ANY)
    bf16 = jnp.bfloat16
    return pl.pallas_call(
        functools.partial(kernel, rng_count, chan_count),
        out_shape=jax.ShapeDtypeStruct((1, own_bins, gates * rng_count), jnp.float32),
        in_specs=[hbm, vmem, vmem, vmem, hbm],
        out_specs=vmem,
        scratch_shapes=[
            pltpu.VMEM((2, rx_count, pulses, gates + LANES), bf16),
            pltpu.VMEM((2 * bins, 2 * bins), bf16),
            pltpu.VMEM((2 * rx_count, beam_count, 2 * chips), jnp.float32),
            pltpu.VMEM((beam_count, rx_count * 2 * chips, 2 * LANES), bf16),
            pltpu.VMEM((2 * per_chunk * pulses, rx_count * 2 * LANES), bf16),
            pltpu.VMEM((chunks, beam_count, 2, pulses, width), bf16),
            pltpu.VMEM((chunks, 2, bins, width), bf16),
            pltpu.VMEM((chunks, rng_count, own_bins * per_chunk, LANES), bf16),
            pltpu.VMEM((chunks, rng_count, own_bins * per_chunk, LANES), bf16),
            pltpu.SemaphoreType.DMA,
            pltpu.SemaphoreType.DMA,
            pltpu.SemaphoreType.DMA((2,)),
            pltpu.SemaphoreType.DMA((chunks,)),
            pltpu.SemaphoreType.DMA((chunks,)),
            pltpu.SemaphoreType.DMA((chunks,)),
            pltpu.SemaphoreType.DMA((chunks,)),
        ],
        compiler_params=pltpu.CompilerParams(
            collective_id=0, has_side_effects=True, vmem_limit_bytes=48 * 2**20
        ),
        cost_estimate=pl.CostEstimate(
            flops=3 * 10**9, bytes_accessed=4 * 2**20, transcendentals=0
        ),
    )(
        samples,
        phase_codes,
        block_pattern,
        steering.reshape(2 * beam_count, pair_count),
        dft_table(bins),
    )


def solution(mesh):
    return jax.shard_map(
        functools.partial(local, mesh.shape["rng"], mesh.shape["chan"]),
        mesh=mesh,
        in_specs=(P(None, None, "chan", "rng"), P(), P(), P()),
        out_specs=P("chan", "rng", None),
        check_vma=False,
    )
```

time: 148 us -> 60.1 us (0.41); the launches traced: 146 us -> 59.8 us
  Pallas kernels: 0 us -> 54 us
  blocking collectives: 45.5 us -> 0 us
  local copies, waits for them, and re-layouts: 49.5 us -> 5.74 us
  other arithmetic: 14.8 us -> 0 us
  matrix products: 12.3 us -> 0 us
  waiting for transfers between devices: 11.7 us -> 0 us
  starting transfers between devices: 11.6 us -> 0 us
    pallas_call x0 -> x1, Pallas kernels: none -> 54 us  [local(): pl.pallas_call(functools.partial(kernel, rng_count, chan_count), out_shap...]
    all_to_all x1 -> x0, blocking collectives: 45.5 us -> none  [local(): lax.all_to_all(spectrum, 'rng', split_axis=2, concat_axis=3, tiled=True)]
    reshape x5 -> x0, local copies, waits for them, and re-layouts: 33.9 us -> none  [the longest x2 31.6 us: local(): matched = matched.reshape(2, rx_count * tx_count, pulse_count, gate_count)]
    dot_general x4 -> x0, matrix products: 12.3 us -> none  [the longest x1 5.02 us: local(): jnp.einsum('rpms,ctsg->crtpmg', stacked, filters, preferred_element_type=...]
    all_to_all x1 -> x0, waiting for transfers between devices: 11.7 us -> none  [local(): lax.all_to_all(beams, 'chan', split_axis=1, concat_axis=2, tiled=True)]
    all_to_all x1 -> x0, starting transfers between devices: 10.3 us -> none  [local(): lax.all_to_all(beams, 'chan', split_axis=1, concat_axis=2, tiled=True)]
    neg x3 -> x0, other arithmetic: 4.96 us -> none  [the longest x1 3.85 us: doppler(): -sine]
    another operation x4 -> x0, local copies, waits for them, and re-layouts: 4.76 us -> none  [banded(): tiled = jnp.tile(period, (1, chip_count))[:, :2 * chip_count * chip_count]]
  transfers between devices with their start and end apart: 2 -> 0, of which waited for: 1 -> 0; matrix products, arithmetic and copies ran while one was open for 16% -> 0% of each run, Pallas kernels for 0% -> 0%
where the time goes in v1:
time: 60.1 us; the launch traced here: 59.8 us
  Pallas kernels  54 us (90%)
  local copies, waits for them, and re-layouts  5.74 us (10%)
    pallas_call x1, Pallas kernels, local(): pl.pallas_call(functools.partial(kernel, rng_count, chan_count), out_shap...  54 us
    unnamed x10, local copies, waits for them, and re-layouts  5.74 us

profile of v1, /device:TPU:1, one launch (start us, length us, event | category | flops | bytes accessed | tf_op | source)
XLA Modules:
  0.0 59.8 jit_solution(12982914617193333235)
XLA Ops:
  0.0 0.8 %copy.6.pattern_ref = s32[16,8]{1,0:T(8,128)S(1)} copy(s32[16,8]{0,1:T(8,128)} %param.7) | data formatting | bytes 1024 | tf_op args[2]
  0.8 0.0 copy-start
  0.8 1.0 %copy-done = bf16[2,4,64,512]{3,2,1,0:T(8,128)(2,1)S(1)} copy-done((bf16[2,4,64,512]{3,2,1,0:T(8,128)(2,1)S(1)}, bf16[2,4,64,512]{3,2,1,0:T(8,128)(2,1)}, u32[]{:S(2)}) %copy-start) | copy-done | bytes 524312
  1.8 0.0 copy-start.1
  1.8 0.7 %copy-done.1 = s32[16,128]{1,0:T(8,128)S(1)} copy-done((s32[16,128]{1,0:T(8,128)S(1)}, s32[16,128]{1,0:T(8,128)}, u32[]{:S(2)}) %copy-start.1) | copy-done | bytes 8216
  2.5 0.0 copy-start.2
  2.5 0.7 %copy-done.2 = bf16[2,8,64]{2,1,0:T(8,128)(2,1)S(1)} copy-done((bf16[2,8,64]{2,1,0:T(8,128)(2,1)S(1)}, bf16[2,8,64]{2,1,0:T(8,128)(2,1)}, u32[]{:S(2)}) %copy-start.2) | copy-done | bytes 2072
  3.2 0.0 copy-start.3
  3.2 1.6 %copy-done.3 = bf16[1024,1024]{1,0:T(8,128)(2,1)S(1)} copy-done((bf16[1024,1024]{1,0:T(8,128)(2,1)S(1)}, bf16[1024,1024]{1,0:T(8,128)(2,1)}, u32[]{:S(2)}) %copy-start.3) | copy-done | bytes 2097176
  4.8 54.0 %shard_map.55 = f32[1,8,32768]{2,1,0:T(8,128)S(1)} custom-call(bf16[2,4,64,512]{3,2,1,0:T(8,128)(2,1)S(1)} %copy-done, s32[16,128]{1,0:T(8,128)S(1)} %copy-done.1, s32[16,8]{1,0:T(8,128)S(1)} %copy.6.pattern_ref, bf16[16,64]{1,0:T(8,128)(2,1)S(1)} %bitcast.1, bf16[1024,1024]{1,0:T(8,128)(2,1)S(1)} %copy-done.3), custom_call_target="tpu_custom_call" | custom-call | flops 3000000000 | bytes 4194304 | tf_op jit(solution)/shard_map/pallas_call | solution.py:280
  58.8 1.0 %copy.8 = f32[1,8,32768]{2,1,0:T(8,128)} copy(f32[1,8,32768]{2,1,0:T(8,128)S(1)} %shard_map.55) | data formatting | bytes 2097152
Async XLA Ops:
  0.8 1.0 %copy-start = (bf16[2,4,64,512]{3,2,1,0:T(8,128)(2,1)S(1)}, bf16[2,4,64,512]{3,2,1,0:T(8,128)(2,1)}, u32[]{:S(2)}) copy-start(bf16[2,4,64,512]{3,2,1,0:T(8,128)(2,1)} %samples_ref.1) | copy-start | bytes 1572868
  1.8 0.7 %copy-start.1 = (s32[16,128]{1,0:T(8,128)S(1)}, s32[16,128]{1,0:T(8,128)}, u32[]{:S(2)}) copy-start(s32[16,128]{1,0:T(8,128)} %codes_ref.1) | copy-start | bytes 24580
  2.5 0.7 %copy-start.2 = (bf16[2,8,64]{2,1,0:T(8,128)(2,1)S(1)}, bf16[2,8,64]{2,1,0:T(8,128)(2,1)}, u32[]{:S(2)}) copy-start(bf16[2,8,64]{2,1,0:T(8,128)(2,1)} %param.8) | copy-start | bytes 6148
  3.2 1.6 %copy-start.3 = (bf16[1024,1024]{1,0:T(8,128)(2,1)S(1)}, bf16[1024,1024]{1,0:T(8,128)(2,1)}, u32[]{:S(2)}) copy-start(bf16[1024,1024]{1,0:T(8,128)(2,1)} %constant.2.clone.table_hbm) | copy-start | bytes 6291460

commit v2 on v1

--- a/solution.py
+++ b/solution.py
@@ -11,6 +11,8 @@
 
 PHASES = 16
 LANES = 128
+BLOCKS = (1, 1, 1, 1)
+VMEM_BYTES = 64 * 2**20 - 2**17
 MESH = pl.DeviceIdType.MESH
 
 
@@ -31,42 +33,53 @@
 def kernel(
     rng_count,
     chan_count,
+    blocks,
     samples_ref,
+    codes_hbm,
+    pattern_hbm,
+    steering_hbm,
+    table_hbm,
+    out_ref,
     codes_ref,
     pattern_ref,
     steering_ref,
-    table_hbm,
-    out_ref,
     extended,
     table,
     taps,
     filters,
     lines,
-    outgoing,
-    gathered,
-    power_out,
-    power_in,
     load_sem,
-    table_sem,
     edge_sem,
     beam_send,
     beam_recv,
     power_send,
     power_recv,
+    *buffers,
 ):
     rng = lax.axis_index("rng")
     chan = lax.axis_index("chan")
     rx_count, pulses, gates = samples_ref.shape[1:]
     chips = codes_ref.shape[1]
-    chunks = outgoing.shape[0]
-    width = outgoing.shape[4]
-    per_chunk = width // LANES
+    chunks = len(blocks)
+    outgoing, gathered, power_out, power_in = (
+        buffers[i * chunks : (i + 1) * chunks] for i in range(4)
+    )
+    starts = [sum(blocks[:i]) for i in range(chunks)]
     bins = table.shape[0] // 2
     own_bins = bins // rng_count
 
-    load = pltpu.make_async_copy(samples_ref, extended.at[:, :, :, pl.ds(0, gates)], load_sem)
+    small = [
+        pltpu.make_async_copy(codes_hbm, codes_ref, load_sem.at[0]),
+        pltpu.make_async_copy(pattern_hbm, pattern_ref, load_sem.at[1]),
+        pltpu.make_async_copy(steering_hbm, steering_ref, load_sem.at[2]),
+    ]
+    for copy in small:
+        copy.start()
+    load = pltpu.make_async_copy(
+        samples_ref, extended.at[:, :, :, pl.ds(0, gates)], load_sem.at[3]
+    )
     load.start()
-    table_load = pltpu.make_async_copy(table_hbm, table, table_sem)
+    table_load = pltpu.make_async_copy(table_hbm, table, load_sem.at[4])
     table_load.start()
 
     barrier = pltpu.get_barrier_semaphore()
@@ -81,12 +94,19 @@
         peer = lax.rem(rng + step, rng_count)
         pl.semaphore_signal(barrier, inc=1, device_id={"rng": peer}, device_id_type=MESH)
 
-    tx_count, block_count = pattern_ref.shape
+    for copy in small:
+        copy.wait()
+    block_count, tx_count = pattern_ref.shape
     spread = (
         lax.broadcasted_iota(jnp.int32, (block_count, chips), 1) // (chips // block_count)
         == lax.broadcasted_iota(jnp.int32, (block_count, chips), 0)
     ).astype(jnp.float32)
-    active = dot(pattern_ref[...].astype(jnp.float32), spread)
+    active = lax.dot_general(
+        pattern_ref[...].astype(jnp.float32),
+        spread,
+        (((0,), (0,)), ((), ())),
+        preferred_element_type=jnp.float32,
+    )
     phase = codes_ref[...].astype(jnp.float32) * (2.0 * math.pi / PHASES)
     code_re = (jnp.cos(phase) * active).astype(jnp.bfloat16)
     code_im = (jnp.sin(phase) * active).astype(jnp.bfloat16)
@@ -115,9 +135,9 @@
 
     def fill_lines(chunk):
         for part in range(2):
-            for block in range(per_chunk):
-                at = (chunk * per_chunk + block) * LANES
-                top = (part * per_chunk + block) * pulses
+            for block in range(blocks[chunk]):
+                at = (starts[chunk] + block) * LANES
+                top = (part * blocks[chunk] + block) * pulses
                 for rx in range(rx_count):
                     lines[pl.ds(top, pulses), pl.ds(rx * 2 * LANES, 2 * LANES)] = extended[
                         part, rx, :, pl.ds(at, 2 * LANES)
@@ -141,16 +161,16 @@
                             pl.ds(part * LANES, LANES),
                         ] = both[2 * rx + part, :, half * LANES : (half + 1) * LANES]
 
-    def form_beam(beam):
-        mixed = dot(lines[...], filters[beam])
-        rows = per_chunk * pulses
+    def form_beam(chunk, beam):
+        rows = blocks[chunk] * pulses
+        mixed = dot(lines[pl.ds(0, 2 * rows), :], filters[beam])
         real = mixed[:rows, :LANES] - mixed[rows:, LANES:]
         imag = mixed[rows:, :LANES] + mixed[:rows, LANES:]
         return real.astype(jnp.bfloat16), imag.astype(jnp.bfloat16)
 
-    def put(target, values, top):
+    def put(chunk, target, values, top):
         for part in range(2):
-            for block in range(per_chunk):
+            for block in range(blocks[chunk]):
                 target[part, pl.ds(top, pulses), pl.ds(block * LANES, LANES)] = values[part][
                     block * pulses : (block + 1) * pulses
                 ]
@@ -159,8 +179,8 @@
 
     def beam_copy(chunk, beam):
         return pltpu.make_async_remote_copy(
-            src_ref=outgoing.at[chunk, beam],
-            dst_ref=gathered.at[chunk, :, mine, :],
+            src_ref=outgoing[chunk].at[beam],
+            dst_ref=gathered[chunk].at[:, mine, :],
             send_sem=beam_send.at[chunk],
             recv_sem=beam_recv.at[chunk],
             device_id={"chan": beam},
@@ -198,17 +218,17 @@
             beam = partner(step)
             if chunk == 0:
                 fill_filter(beam)
-            put(outgoing.at[chunk, beam], form_beam(beam), 0)
+            put(chunk, outgoing[chunk].at[beam], form_beam(chunk, beam), 0)
             beam_copy(chunk, beam).start()
 
         if chunk == 0:
             fill_filter(chan)
-        put(gathered.at[chunk], form_beam(chan), pl.multiple_of(chan * pulses, pulses))
+        put(chunk, gathered[chunk], form_beam(chunk, chan), pl.multiple_of(chan * pulses, pulses))
 
     def power_copy(chunk, peer):
         return pltpu.make_async_remote_copy(
-            src_ref=power_out.at[chunk, peer],
-            dst_ref=power_in.at[chunk, rng],
+            src_ref=power_out[chunk].at[peer],
+            dst_ref=power_in[chunk].at[rng],
             send_sem=power_send.at[chunk],
             recv_sem=power_recv.at[chunk],
             device_id={"rng": peer},
@@ -218,19 +238,21 @@
     table_load.wait()
     step_bins = 128
     for chunk in range(chunks):
-        arrived = outgoing.at[chunk, pl.ds(0, chan_count - 1)]
+        arrived = outgoing[chunk].at[pl.ds(0, chan_count - 1)]
         pltpu.make_async_copy(arrived, arrived, beam_recv.at[chunk]).wait()
-        series = jnp.concatenate([gathered[chunk, 0], gathered[chunk, 1]], axis=0)
+        series = jnp.concatenate([gathered[chunk][0], gathered[chunk][1]], axis=0)
         for at in range(0, bins, step_bins):
             real = dot(table[pl.ds(at, step_bins), :], series)
             imag = dot(table[pl.ds(bins + at, step_bins), :], series)
             real = real.astype(jnp.bfloat16).astype(jnp.float32)
             imag = imag.astype(jnp.bfloat16).astype(jnp.float32)
-            power = (real * real + imag * imag).reshape(step_bins // own_bins, own_bins, width)
+            power = (real * real + imag * imag).reshape(
+                step_bins // own_bins, own_bins, blocks[chunk] * LANES
+            )
             power = jnp.concatenate(
-                [power[:, :, i * LANES : (i + 1) * LANES] for i in range(per_chunk)], axis=1
+                [power[:, :, i * LANES : (i + 1) * LANES] for i in range(blocks[chunk])], axis=1
             )
-            power_out[chunk, pl.ds(at // own_bins, step_bins // own_bins)] = power.astype(
+            power_out[chunk][pl.ds(at // own_bins, step_bins // own_bins)] = power.astype(
                 jnp.bfloat16
             )
 
@@ -238,30 +260,29 @@
         def _(step):
             power_copy(chunk, lax.rem(rng + step, rng_count)).start()
 
-        power_in[chunk, rng] = power_out[chunk, rng]
+        power_in[chunk][rng] = power_out[chunk][rng]
 
     total = jnp.zeros((own_bins, LANES), jnp.float32)
     for chunk in range(chunks):
-        arrived = power_in.at[chunk, pl.ds(0, rng_count - 1)]
+        arrived = power_in[chunk].at[pl.ds(0, rng_count - 1)]
         pltpu.make_async_copy(arrived, arrived, power_recv.at[chunk]).wait()
-        level = power_in[chunk].astype(jnp.float32)
-        level = jnp.sum(level, axis=0)
-        for i in range(per_chunk):
+        level = jnp.sum(power_in[chunk][...].astype(jnp.float32), axis=0)
+        for i in range(blocks[chunk]):
             total = total + level[i * own_bins : (i + 1) * own_bins]
     average = jnp.sum(total, axis=1, keepdims=True) / float(rng_count * gates)
     scale = 1.0 / (average + 1e-06)
     for source in range(rng_count):
         for chunk in range(chunks):
-            level = power_in[chunk, source].astype(jnp.float32)
-            for i in range(per_chunk):
+            level = power_in[chunk][source].astype(jnp.float32)
+            for i in range(blocks[chunk]):
                 out_ref[
-                    0, :, pl.ds(source * gates + chunk * width + i * LANES, LANES)
+                    0, :, pl.ds(source * gates + (starts[chunk] + i) * LANES, LANES)
                 ] = level[i * own_bins : (i + 1) * own_bins] * scale
 
     for chunk in range(chunks):
-        sent = outgoing.at[chunk, pl.ds(0, chan_count - 1)]
+        sent = outgoing[chunk].at[pl.ds(0, chan_count - 1)]
         pltpu.make_async_copy(sent, sent, beam_send.at[chunk]).wait()
-        sent = power_out.at[chunk, pl.ds(0, rng_count - 1)]
+        sent = power_out[chunk].at[pl.ds(0, rng_count - 1)]
         pltpu.make_async_copy(sent, sent, power_send.at[chunk]).wait()
 
 
@@ -271,37 +292,37 @@
     _, beam_count, pair_count = steering.shape
     bins = pulses * chan_count
     own_bins = bins // rng_count
-    chunks = 2
-    width = gates // chunks
-    per_chunk = width // LANES
+    blocks = BLOCKS
+    chunks = len(blocks)
     vmem = pl.BlockSpec(memory_space=pltpu.VMEM)
-    hbm = pl.BlockSpec(memory_space=pl.ANY)
+    hbm = pl.BlockSpec(memory_space=pltpu.HBM)
     bf16 = jnp.bfloat16
     return pl.pallas_call(
-        functools.partial(kernel, rng_count, chan_count),
+        functools.partial(kernel, rng_count, chan_count, blocks),
         out_shape=jax.ShapeDtypeStruct((1, own_bins, gates * rng_count), jnp.float32),
-        in_specs=[hbm, vmem, vmem, vmem, hbm],
+        in_specs=[hbm] * 5,
         out_specs=vmem,
         scratch_shapes=[
+            pltpu.VMEM(phase_codes.shape, jnp.int32),
+            pltpu.VMEM(block_pattern.shape[::-1], jnp.int32),
+            pltpu.VMEM((2 * beam_count, pair_count), bf16),
             pltpu.VMEM((2, rx_count, pulses, gates + LANES), bf16),
             pltpu.VMEM((2 * bins, 2 * bins), bf16),
             pltpu.VMEM((2 * rx_count, beam_count, 2 * chips), jnp.float32),
             pltpu.VMEM((beam_count, rx_count * 2 * chips, 2 * LANES), bf16),
-            pltpu.VMEM((2 * per_chunk * pulses, rx_count * 2 * LANES), bf16),
-            pltpu.VMEM((chunks, beam_count, 2, pulses, width), bf16),
-            pltpu.VMEM((chunks, 2, bins, width), bf16),
-            pltpu.VMEM((chunks, rng_count, own_bins * per_chunk, LANES), bf16),
-            pltpu.VMEM((chunks, rng_count, own_bins * per_chunk, LANES), bf16),
-            pltpu.SemaphoreType.DMA,
-            pltpu.SemaphoreType.DMA,
+            pltpu.VMEM((2 * max(blocks) * pulses, rx_count * 2 * LANES), bf16),
+            pltpu.SemaphoreType.DMA((5,)),
             pltpu.SemaphoreType.DMA((2,)),
             pltpu.SemaphoreType.DMA((chunks,)),
             pltpu.SemaphoreType.DMA((chunks,)),
             pltpu.SemaphoreType.DMA((chunks,)),
             pltpu.SemaphoreType.DMA((chunks,)),
+            *(pltpu.VMEM((beam_count, 2, pulses, n * LANES), bf16) for n in blocks),
+            *(pltpu.VMEM((2, bins, n * LANES), bf16) for n in blocks),
+            *(pltpu.VMEM((rng_count, own_bins * n, LANES), bf16) for n in blocks * 2),
         ],
         compiler_params=pltpu.CompilerParams(
-            collective_id=0, has_side_effects=True, vmem_limit_bytes=48 * 2**20
+            collective_id=0, has_side_effects=True, vmem_limit_bytes=VMEM_BYTES
         ),
         cost_estimate=pl.CostEstimate(
             flops=3 * 10**9, bytes_accessed=4 * 2**20, transcendentals=0
@@ -309,7 +330,7 @@
     )(
         samples,
         phase_codes,
-        block_pattern,
+        block_pattern.T,
         steering.reshape(2 * beam_count, pair_count),
         dft_table(bins),
     )

time: 60.1 us -> 54.8 us (0.912)
  local copies, waits for them, and re-layouts: 5.74 us -> 2.26 us
  Pallas kernels: 54 us -> 52.4 us
    unnamed x10 -> x1, local copies, waits for them, and re-layouts: 5.74 us -> 2.26 us
    pallas_call x1, Pallas kernels: 54 us -> 52.4 us  [local(): pl.pallas_call(functools.partial(kernel, rng_count, chan_count, blocks),...]
where the time goes in v2:
time: 54.8 us; the launch traced here: 54.7 us
  Pallas kernels  52.4 us (96%)
  local copies, waits for them, and re-layouts  2.26 us (4%)
    pallas_call x1, Pallas kernels, local(): pl.pallas_call(functools.partial(kernel, rng_count, chan_count, blocks),...  52.4 us
    unnamed x1, local copies, waits for them, and re-layouts  2.26 us

profile of v2, /device:TPU:1, one launch (start us, length us, event | category | flops | bytes accessed | tf_op | source)
XLA Modules:
  0.0 54.7 jit_solution(10237054637566880357)
XLA Ops:
  0.0 52.4 %shard_map.55 = f32[1,8,32768]{2,1,0:T(8,128)} custom-call(bf16[2,4,64,512]{3,2,1,0:T(8,128)(2,1)} %samples_ref.1, s32[16,128]{1,0:T(8,128)} %codes_hbm.1, s32[8,16]{1,0:T(8,128)} %bitcast.2, bf16[16,64]{1,0:T(8,128)(2,1)} %bitcast.3, bf16[1024,1024]{1,0:T(8,128)(2,1)} %constant.2.clone.table_hbm), custom_call_target="tpu_custom_call" | custom-call | flops 3000000000 | bytes 4194304 | tf_op jit(solution)/shard_map/pallas_call | solution.py:300
  52.4 2.3 %copy.7 = f32[1,8,32768]{2,1,0:T(8,128)} copy(f32[1,8,32768]{2,1,0:T(8,128)} %shard_map.55) | data formatting | bytes 2097152

commit v3 on v2

--- a/solution.py
+++ b/solution.py
@@ -12,6 +12,7 @@
 PHASES = 16
 LANES = 128
 BLOCKS = (1, 1, 1, 1)
+STEPS = 2
 VMEM_BYTES = 64 * 2**20 - 2**17
 MESH = pl.DeviceIdType.MESH
 
@@ -39,23 +40,28 @@
     pattern_hbm,
     steering_hbm,
     table_hbm,
-    out_ref,
-    codes_ref,
-    pattern_ref,
-    steering_ref,
-    extended,
-    table,
-    taps,
-    filters,
-    lines,
-    load_sem,
-    edge_sem,
-    beam_send,
-    beam_recv,
-    power_send,
-    power_recv,
-    *buffers,
+    *refs,
 ):
+    levels, scale_hbm = refs[: len(blocks)], refs[len(blocks)]
+    (
+        codes_ref,
+        pattern_ref,
+        steering_ref,
+        extended,
+        table,
+        taps,
+        filters,
+        lines,
+        load_sem,
+        edge_sem,
+        beam_send,
+        beam_recv,
+        power_send,
+        power_recv,
+        scale,
+        scale_sem,
+        *buffers,
+    ) = refs[len(blocks) + 1 :]
     rng = lax.axis_index("rng")
     chan = lax.axis_index("chan")
     rx_count, pulses, gates = samples_ref.shape[1:]
@@ -256,7 +262,7 @@
                 jnp.bfloat16
             )
 
-        @pl.loop(1, rng_count)
+        @pl.loop(1, rng_count, unroll=7)
         def _(step):
             power_copy(chunk, lax.rem(rng + step, rng_count)).start()
 
@@ -266,24 +272,35 @@
     for chunk in range(chunks):
         arrived = power_in[chunk].at[pl.ds(0, rng_count - 1)]
         pltpu.make_async_copy(arrived, arrived, power_recv.at[chunk]).wait()
+        pltpu.make_async_copy(power_in[chunk], levels[chunk], load_sem.at[chunk]).start()
         level = jnp.sum(power_in[chunk][...].astype(jnp.float32), axis=0)
         for i in range(blocks[chunk]):
             total = total + level[i * own_bins : (i + 1) * own_bins]
     average = jnp.sum(total, axis=1, keepdims=True) / float(rng_count * gates)
-    scale = 1.0 / (average + 1e-06)
-    for source in range(rng_count):
-        for chunk in range(chunks):
-            level = power_in[chunk][source].astype(jnp.float32)
-            for i in range(blocks[chunk]):
-                out_ref[
-                    0, :, pl.ds(source * gates + (starts[chunk] + i) * LANES, LANES)
-                ] = level[i * own_bins : (i + 1) * own_bins] * scale
-
+    scale[...] = jnp.broadcast_to(1.0 / (average + 1e-06), scale.shape)
+    scale_store = pltpu.make_async_copy(scale, scale_hbm, scale_sem)
+    scale_store.start()
     for chunk in range(chunks):
         sent = outgoing[chunk].at[pl.ds(0, chan_count - 1)]
         pltpu.make_async_copy(sent, sent, beam_send.at[chunk]).wait()
         sent = power_out[chunk].at[pl.ds(0, rng_count - 1)]
         pltpu.make_async_copy(sent, sent, power_send.at[chunk]).wait()
+        pltpu.make_async_copy(power_in[chunk], levels[chunk], load_sem.at[chunk]).wait()
+    scale_store.wait()
+
+
+def finish(blocks, *refs):
+    levels, scale_ref, out_ref = refs[:-2], refs[-2], refs[-1]
+    sources, _, lanes = levels[0].shape
+    own_bins = out_ref.shape[1]
+    scale = scale_ref[...]
+    at = 0
+    for source in range(sources):
+        for n, ref in zip(blocks, levels, strict=True):
+            level = ref[source].astype(jnp.float32)
+            for i in range(n):
+                out_ref[0, :, pl.ds(at, lanes)] = level[i * own_bins : (i + 1) * own_bins] * scale
+                at += lanes
 
 
 def local(rng_count, chan_count, samples, phase_codes, block_pattern, steering):
@@ -297,11 +314,14 @@
     vmem = pl.BlockSpec(memory_space=pltpu.VMEM)
     hbm = pl.BlockSpec(memory_space=pltpu.HBM)
     bf16 = jnp.bfloat16
-    return pl.pallas_call(
+    levels = pl.pallas_call(
         functools.partial(kernel, rng_count, chan_count, blocks),
-        out_shape=jax.ShapeDtypeStruct((1, own_bins, gates * rng_count), jnp.float32),
+        out_shape=[
+            jax.ShapeDtypeStruct((rng_count, own_bins * n, LANES), bf16) for n in blocks
+        ]
+        + [jax.ShapeDtypeStruct((own_bins, LANES), jnp.float32)],
         in_specs=[hbm] * 5,
-        out_specs=vmem,
+        out_specs=[hbm] * (chunks + 1),
         scratch_shapes=[
             pltpu.VMEM(phase_codes.shape, jnp.int32),
             pltpu.VMEM(block_pattern.shape[::-1], jnp.int32),
@@ -317,6 +337,8 @@
             pltpu.SemaphoreType.DMA((chunks,)),
             pltpu.SemaphoreType.DMA((chunks,)),
             pltpu.SemaphoreType.DMA((chunks,)),
+            pltpu.VMEM((own_bins, LANES), jnp.float32),
+            pltpu.SemaphoreType.DMA,
             *(pltpu.VMEM((beam_count, 2, pulses, n * LANES), bf16) for n in blocks),
             *(pltpu.VMEM((2, bins, n * LANES), bf16) for n in blocks),
             *(pltpu.VMEM((rng_count, own_bins * n, LANES), bf16) for n in blocks * 2),
@@ -334,6 +356,17 @@
         steering.reshape(2 * beam_count, pair_count),
         dft_table(bins),
     )
+    return pl.pallas_call(
+        functools.partial(finish, blocks),
+        out_shape=jax.ShapeDtypeStruct((1, own_bins, gates * rng_count), jnp.float32),
+        grid=(STEPS,),
+        in_specs=[
+            pl.BlockSpec((rng_count // STEPS, own_bins * n, LANES), lambda i: (i, 0, 0))
+            for n in blocks
+        ]
+        + [pl.BlockSpec((own_bins, LANES), lambda i: (0, 0))],
+        out_specs=pl.BlockSpec((1, own_bins, gates * rng_count // STEPS), lambda i: (0, 0, i)),
+    )(*levels)
 
 
 def solution(mesh):

time: 54.8 us -> 53.7 us (0.980)
  local copies, waits for them, and re-layouts: 2.26 us -> 0 us
  Pallas kernels: 52.4 us -> 53.5 us
    unnamed x1 -> x0, local copies, waits for them, and re-layouts: 2.26 us -> none
    pallas_call x0 -> x1, Pallas kernels: none -> 1.96 us  [local(): pl.pallas_call(functools.partial(finish, blocks), out_shape=jax.ShapeDtyp...]
    pallas_call x1, Pallas kernels: 52.4 us -> 51.5 us  [local(): pl.pallas_call(functools.partial(kernel, rng_count, chan_count, blocks),...]
where the time goes in v3:
time: 53.7 us; the launch traced here: 53.5 us
  Pallas kernels  53.5 us (100%)
    pallas_call x1, Pallas kernels, local(): pl.pallas_call(functools.partial(kernel, rng_count, chan_count, blocks),...  51.5 us
    pallas_call x1, Pallas kernels, local(): pl.pallas_call(functools.partial(finish, blocks), out_shape=jax.ShapeDtyp...  1.96 us

profile of v3, /device:TPU:1, one launch (start us, length us, event | category | flops | bytes accessed | tf_op | source)
XLA Modules:
  0.0 53.5 jit_solution(17577141546949246362)
XLA Ops:
  0.0 51.5 %shard_map.55 = (bf16[64,8,128]{2,1,0:T(8,128)(2,1)}, bf16[64,8,128]{2,1,0:T(8,128)(2,1)}, bf16[64,8,128]{2,1,0:T(8,128)(2,1)}, bf16[64,8,128]{2,1,0:T(8,128)(2,1)}, f32[8,128]{1,0:T(8,128)}) custom-call(bf16[2,4,64,512]{3,2,1,0:T(8,128)(2,1)} %samples_ref.1, s32[16,128]{1,0:T(8,128)} %codes_hbm.1, s32[8,16]{1,0:T(8,128)} %bitcast.2, ...), custom_call_target="tpu_custom_call" | custom-call | flops 3000000000 | bytes 4194304 | tf_op jit(solution)/shard_map/pallas_call | solution.py:317
  51.6 2.0 %shard_map.56 = f32[1,8,32768]{2,1,0:T(8,128)} custom-call(bf16[64,8,128]{2,1,0:T(8,128)(2,1)} %get-tuple-element.10.refs_0_, bf16[64,8,128]{2,1,0:T(8,128)(2,1)} %get-tuple-element.11.refs_1_, bf16[64,8,128]{2,1,0:T(8,128)(2,1)} %get-tuple-element.12.refs_2_, bf16[64,8,128]{2,1,0:T(8,128)(2,1)} %get-tuple-element.13.refs_3_, f32[8,128]{1,0:T(8,128)} %get-tuple-element.14.refs_4_), custom_call_target="tpu_custom_call" | custom-call | tf_op jit(solution)/shard_map/pallas_call | solution.py:359

commit v4 on v3

--- a/solution.py
+++ b/solution.py
@@ -194,7 +194,10 @@
         )
 
     def partner(step):
-        return lax.rem(chan // 2 + step % 4, chan_count // 2) * 2 + (chan + step // 4) % 2
+        pair = (step - 1) // 2
+        turn = jnp.where(pair == 0, 1, jnp.where(pair == 1, 3, jnp.where(pair == 2, 2, 0)))
+        flip = jnp.where(pair == 3, 1, (step - 1) % 2)
+        return lax.rem(chan // 2 + turn, chan_count // 2) * 2 + (chan + flip) % 2
 
     fill_lines(0)
     pl.semaphore_wait(barrier, rng_count + chan_count - 2)

time: 53.7 us -> 53.9 us (level)
  no operation moved by 1% of the time
where the time goes in v4:
time: 53.9 us; the launch traced here: 53.7 us
  Pallas kernels  53.7 us (100%)
    pallas_call x1, Pallas kernels, local(): pl.pallas_call(functools.partial(kernel, rng_count, chan_count, blocks),...  51.8 us
    pallas_call x1, Pallas kernels, local(): pl.pallas_call(functools.partial(finish, blocks), out_shape=jax.ShapeDtyp...  1.96 us

profile of v4, /device:TPU:1, one launch (start us, length us, event | category | flops | bytes accessed | tf_op | source)
XLA Modules:
  0.0 53.7 jit_solution(10394419751073644238)
XLA Ops:
  0.0 51.8 %shard_map.55 = (bf16[64,8,128]{2,1,0:T(8,128)(2,1)}, bf16[64,8,128]{2,1,0:T(8,128)(2,1)}, bf16[64,8,128]{2,1,0:T(8,128)(2,1)}, bf16[64,8,128]{2,1,0:T(8,128)(2,1)}, f32[8,128]{1,0:T(8,128)}) custom-call(bf16[2,4,64,512]{3,2,1,0:T(8,128)(2,1)} %samples_ref.1, s32[16,128]{1,0:T(8,128)} %codes_hbm.1, s32[8,16]{1,0:T(8,128)} %bitcast.2, ...), custom_call_target="tpu_custom_call" | custom-call | flops 3000000000 | bytes 4194304 | tf_op jit(solution)/shard_map/pallas_call | solution.py:320
  51.8 2.0 %shard_map.56 = f32[1,8,32768]{2,1,0:T(8,128)} custom-call(bf16[64,8,128]{2,1,0:T(8,128)(2,1)} %get-tuple-element.10.refs_0_, bf16[64,8,128]{2,1,0:T(8,128)(2,1)} %get-tuple-element.11.refs_1_, bf16[64,8,128]{2,1,0:T(8,128)(2,1)} %get-tuple-element.12.refs_2_, bf16[64,8,128]{2,1,0:T(8,128)(2,1)} %get-tuple-element.13.refs_3_, f32[8,128]{1,0:T(8,128)} %get-tuple-element.14.refs_4_), custom_call_target="tpu_custom_call" | custom-call | tf_op jit(solution)/shard_map/pallas_call | solution.py:362

commit v5 on v3

--- a/solution.py
+++ b/solution.py
@@ -21,9 +21,7 @@
     index = np.arange(pulse_count)
     angles = (np.outer(index, index) % pulse_count) * (2.0 * math.pi / pulse_count)
     cosine, sine = np.cos(angles), np.sin(angles)
-    table = np.concatenate(
-        [np.concatenate([cosine, sine], axis=1), np.concatenate([-sine, cosine], axis=1)]
-    )
+    table = np.concatenate([cosine, sine], axis=1)
     return jnp.asarray(table, jnp.bfloat16)
 
 
@@ -71,7 +69,7 @@
         buffers[i * chunks : (i + 1) * chunks] for i in range(4)
     )
     starts = [sum(blocks[:i]) for i in range(chunks)]
-    bins = table.shape[0] // 2
+    bins = table.shape[0]
     own_bins = bins // rng_count
 
     small = [
@@ -246,10 +244,18 @@
     for chunk in range(chunks):
         arrived = outgoing[chunk].at[pl.ds(0, chan_count - 1)]
         pltpu.make_async_copy(arrived, arrived, beam_recv.at[chunk]).wait()
-        series = jnp.concatenate([gathered[chunk][0], gathered[chunk][1]], axis=0)
+        part_re, part_im = gathered[chunk][0], gathered[chunk][1]
+        series = jnp.concatenate(
+            [
+                jnp.concatenate([part_re, part_im], axis=1),
+                jnp.concatenate([part_im, -part_re], axis=1),
+            ],
+            axis=0,
+        )
+        width = blocks[chunk] * LANES
         for at in range(0, bins, step_bins):
-            real = dot(table[pl.ds(at, step_bins), :], series)
-            imag = dot(table[pl.ds(bins + at, step_bins), :], series)
+            mixed = dot(table[pl.ds(at, step_bins), :], series)
+            real, imag = mixed[:, :width], mixed[:, width:]
             real = real.astype(jnp.bfloat16).astype(jnp.float32)
             imag = imag.astype(jnp.bfloat16).astype(jnp.float32)
             power = (real * real + imag * imag).reshape(
@@ -327,7 +333,7 @@
             pltpu.VMEM(block_pattern.shape[::-1], jnp.int32),
             pltpu.VMEM((2 * beam_count, pair_count), bf16),
             pltpu.VMEM((2, rx_count, pulses, gates + LANES), bf16),
-            pltpu.VMEM((2 * bins, 2 * bins), bf16),
+            pltpu.VMEM((bins, 2 * bins), bf16),
             pltpu.VMEM((2 * rx_count, beam_count, 2 * chips), jnp.float32),
             pltpu.VMEM((beam_count, rx_count * 2 * chips, 2 * LANES), bf16),
             pltpu.VMEM((2 * max(blocks) * pulses, rx_count * 2 * LANES), bf16),

time: 53.7 us -> 53.7 us (level)
  no operation moved by 1% of the time
where the time goes in v5:
time: 53.7 us; the launch traced here: 53.5 us
  Pallas kernels  53.5 us (100%)
    pallas_call x1, Pallas kernels, local(): pl.pallas_call(functools.partial(kernel, rng_count, chan_count, blocks),...  51.6 us
    pallas_call x1, Pallas kernels, local(): pl.pallas_call(functools.partial(finish, blocks), out_shape=jax.ShapeDtyp...  1.96 us

profile of v5, /device:TPU:1, one launch (start us, length us, event | category | flops | bytes accessed | tf_op | source)
XLA Modules:
  0.0 53.5 jit_solution(12109129828834271407)
XLA Ops:
  0.0 51.6 %shard_map.55 = (bf16[64,8,128]{2,1,0:T(8,128)(2,1)}, bf16[64,8,128]{2,1,0:T(8,128)(2,1)}, bf16[64,8,128]{2,1,0:T(8,128)(2,1)}, bf16[64,8,128]{2,1,0:T(8,128)(2,1)}, f32[8,128]{1,0:T(8,128)}) custom-call(bf16[2,4,64,512]{3,2,1,0:T(8,128)(2,1)} %samples_ref.1, s32[16,128]{1,0:T(8,128)} %codes_hbm.1, s32[8,16]{1,0:T(8,128)} %bitcast.2, ...), custom_call_target="tpu_custom_call" | custom-call | flops 3000000000 | bytes 4194304 | tf_op jit(solution)/shard_map/pallas_call | solution.py:323
  51.6 2.0 %shard_map.56 = f32[1,8,32768]{2,1,0:T(8,128)} custom-call(bf16[64,8,128]{2,1,0:T(8,128)(2,1)} %get-tuple-element.10.refs_0_, bf16[64,8,128]{2,1,0:T(8,128)(2,1)} %get-tuple-element.11.refs_1_, bf16[64,8,128]{2,1,0:T(8,128)(2,1)} %get-tuple-element.12.refs_2_, bf16[64,8,128]{2,1,0:T(8,128)(2,1)} %get-tuple-element.13.refs_3_, f32[8,128]{1,0:T(8,128)} %get-tuple-element.14.refs_4_), custom_call_target="tpu_custom_call" | custom-call | tf_op jit(solution)/shard_map/pallas_call | solution.py:365
